TPU v7x, 32 devices: a whole 2x2x4 slice. The times are simulated.
32 devices in a mesh: ctx: 8 (over z, x), tp: 4 (over y, core).
Axes of the slice: x: 2, y: 2, z: 4, core: 2. Of those that a mesh axis runs over, the one named last changes fastest.
Arguments:
- tokens: bfloat16 [4096, 4096], P('ctx', 'tp'), may hold values from -16 to 16
- query_weight: bfloat16 [4096, 4096], P(None, 'tp'), may hold values from -0.09375 to 0.09375
- key_weight: bfloat16 [4096, 1024], P(None, 'tp'), may hold values from -0.09375 to 0.09375
- value_weight: bfloat16 [4096, 1024], P(None, 'tp'), may hold values from -0.09375 to 0.09375
- out_weight: bfloat16 [4096, 4096], P('tp'), may hold values from -0.09375 to 0.09375
- links: int32 [32, 16], P('ctx'), may hold values from 0 to 31, as said below
- counts: int32 [32], P('ctx'), may hold values from 1 to 16, as said below
- doc_ids: int32 [32], replicated, may hold values from 0 to 7, never falling along the last dimension, each value on 1 to 8 neighbouring positions
Outputs:
- mixed: bfloat16 [4096, 4096], P(('ctx', 'tp'))
Inputs may be any that keep to these rules, and one draw needn't show every extreme that they name: `links`: the first entry of each row is the query block itself; the entries of a row are distinct; every listed block lies within 4 ctx indices of its query block (block index // 4), and some query block of every ctx index lists a block exactly 4 indices away. `counts`: the first query block of each ctx index has 2 or more live slots, and block 0 has 16.
All inputs are finite; a program needn't handle non-finite values.
Results may differ from a plain program's by a relative error of at most 0.017.
Values may be sent and summed in bfloat16 or wider, within the bound.
A program may use at most 128 MiB of HBM per device.

v0:
```python
import jax
import jax.numpy as jnp
from jax import lax
from jax.sharding import PartitionSpec as P

HEAD_DIM = 128
BLOCK = 128
LINKS = 16
REACH = 4


def from_behind(block, axis, distance):
    devices = range(lax.axis_size(axis))
    route = [(i - distance, i) for i in devices if i - distance in devices]
    return lax.ppermute(block, axis, route)


def local(tokens, query_weight, key_weight, value_weight, out_weight, links, counts, doc_ids):
    row_count = tokens.shape[0]
    query_width = query_weight.shape[1]
    key_width = key_weight.shape[1]
    piece = lax.all_gather(tokens, "tp", axis=1, tiled=True)
    weights = (query_weight, key_weight, value_weight)
    query, keys, values = tuple(
        (jnp.dot(piece, weight, preferred_element_type=jnp.float32) for weight in weights)
    )
    query = query.astype(jnp.bfloat16)
    block_count = row_count // BLOCK
    stacked = (
        jnp.stack([keys, values]).astype(jnp.bfloat16).reshape(2, block_count, BLOCK, key_width)
    )
    position = lax.axis_index("ctx")
    first_block = position * block_count
    pieces = []
    for offset in range(-REACH, REACH + 1):
        if offset == 0:
            pieces.append(stacked)
        else:
            pieces.append(from_behind(stacked, "ctx", -offset))
    source = jnp.concatenate(pieces, axis=1)
    anchor = (position - REACH) * block_count
    chosen = jnp.take(source, links - anchor, axis=1, mode="clip")
    kv_local = key_width // HEAD_DIM
    group = query_width // key_width
    chosen_keys = chosen[0].reshape(block_count, LINKS, BLOCK, kv_local, HEAD_DIM)
    chosen_values = chosen[1].reshape(block_count, LINKS, BLOCK, kv_local, HEAD_DIM)
    query_blocks = query.reshape(block_count, BLOCK, kv_local, group, HEAD_DIM)
    block_total = doc_ids.shape[0]
    table = jnp.arange(block_total, dtype=jnp.int32)
    query_index = first_block + jnp.arange(block_count, dtype=jnp.int32)[:, None]
    doc_key = jnp.sum(jnp.where(links[:, :, None] == table, doc_ids, 0), axis=-1)
    doc_query = jnp.sum(jnp.where(query_index == table[None, :], doc_ids[None, :], 0), axis=-1)[
        :, None
    ]
    live = jnp.arange(LINKS, dtype=jnp.int32)[None, :] < counts[:, None]
    earlier = (links < query_index) | (doc_key != doc_query)
    same = links == query_index
    causal = jnp.arange(BLOCK)[None, :] <= jnp.arange(BLOCK)[:, None]
    allowed = live[:, None, :, None] & (
        earlier[:, None, :, None] | same[:, None, :, None] & causal[None, :, None, :]
    )
    allowed = allowed[:, None, None]
    scores = jnp.einsum(
        "bqhgd,bskhd->bhgqsk", query_blocks, chosen_keys, preferred_element_type=jnp.float32
    ) * HEAD_DIM ** (-0.5)
    scores = jnp.where(allowed, scores, -1e30)
    top = jnp.max(scores, axis=(4, 5), keepdims=True)
    powers = jnp.where(allowed, jnp.exp(scores - top), 0.0)
    total = jnp.sum(powers, axis=(4, 5), keepdims=True)
    weights = (powers / total).astype(jnp.bfloat16)
    attended = jnp.einsum(
        "bhgqsk,bskhd->bqhgd", weights, chosen_values, preferred_element_type=jnp.float32
    )
    attended = attended.astype(jnp.bfloat16).reshape(row_count, query_width)
    return lax.psum_scatter(
        jnp.dot(attended, out_weight, preferred_element_type=jnp.float32).astype(jnp.bfloat16),
        "tp",
        scatter_dimension=0,
        tiled=True,
    )


def solution(mesh):
    placed = (
        P("ctx", "tp"),
        P(None, "tp"),
        P(None, "tp"),
        P(None, "tp"),
        P("tp", None),
        P("ctx", None),
        P("ctx"),
        P(),
    )
    return jax.shard_map(
        local, mesh=mesh, in_specs=placed, out_specs=P(("ctx", "tp"), None), check_vma=False
    )
```

profile of v0, /device:TPU:6, one launch (start us, length us, event | category | flops | bytes accessed | tf_op | source)
XLA Modules:
  0.0 309.5 jit_solution(8008168904110822595)
XLA Ops:
  13.1 30.6 %all-gather.2.cloned.1.call-done = bf16[512,4096]{1,0:T(8,128)(2,1)} async-done(((bf16[512,1024]{1,0:T(8,128)(2,1)}), bf16[512,4096]{1,0:T(8,128)(2,1)}) %all-gather.2.cloned.1.call-update) | async-done | bytes 4194320 | tf_op jit(solution)/shard_map/all_gather | solution.py:22
  43.7 3.6 %convolution_convert_fusion.2 = bf16[512,256]{1,0:T(8,128)(2,1)S(1)} fusion(bf16[512,4096]{1,0:T(8,128)(2,1)} %all-gather.2.cloned.1.call-done, bf16[4096,256]{1,0:T(8,128)(2,1)S(1)} %copy-done), kind=kOutput, calls=%fused_computation.16 | convolution fusion | flops 1073872896 | bytes 6553600 | tf_op jit(solution)/shard_map/dot_general | solution.py:25
  47.3 3.6 %convolution_convert_fusion.3 = bf16[512,256]{1,0:T(8,128)(2,1)S(1)} fusion(bf16[512,4096]{1,0:T(8,128)(2,1)} %all-gather.2.cloned.1.call-done, bf16[4096,256]{1,0:T(8,128)(2,1)S(1)} %copy-done.4), kind=kOutput, calls=%fused_computation.17 | convolution fusion | flops 1073872896 | bytes 6553600 | tf_op jit(solution)/shard_map/dot_general | solution.py:25
  53.1 3.4 %collective-permute-start.3 = (bf16[2,4,128,256]{3,2,1,0:T(8,128)(2,1)}, bf16[2,4,128,256]{3,2,1,0:T(8,128)(2,1)}, u32[]{:S(2)}, u32[]{:S(2)}) collective-permute-start(bf16[2,4,128,256]{3,2,1,0:T(8,128)(2,1)} %pad_maximum_fusion), channel_id=1, source_target_pairs={{0,4},{4,8},{8,12},{12,16},{16,20},{20,24},{24,28},{1,5},{5,9},{9,... | collective-permute-start | bytes 1572872 | tf_op jit(solution)/shard_map/ppermute | solution.py:15
  56.5 5.9 %collective-permute-start.2 = (bf16[2,4,128,256]{3,2,1,0:T(8,128)(2,1)}, bf16[2,4,128,256]{3,2,1,0:T(8,128)(2,1)}, u32[]{:S(2)}, u32[]{:S(2)}) collective-permute-start(bf16[2,4,128,256]{3,2,1,0:T(8,128)(2,1)} %pad_maximum_fusion), channel_id=1, source_target_pairs={{0,8},{4,12},{8,16},{12,20},{16,24},{20,28},{1,9},{5,13},{9,17},{1... | collective-permute-start | bytes 1572872 | tf_op jit(solution)/shard_map/ppermute | solution.py:15
  62.4 4.5 %collective-permute-start.1 = (bf16[2,4,128,256]{3,2,1,0:T(8,128)(2,1)}, bf16[2,4,128,256]{3,2,1,0:T(8,128)(2,1)}, u32[]{:S(2)}, u32[]{:S(2)}) collective-permute-start(bf16[2,4,128,256]{3,2,1,0:T(8,128)(2,1)} %pad_maximum_fusion), channel_id=1, source_target_pairs={{0,12},{4,16},{8,20},{12,24},{16,28},{1,13},{5,17},{9,21},{13,25},... | collective-permute-start | bytes 1572872 | tf_op jit(solution)/shard_map/ppermute | solution.py:15
  66.9 2.1 collective-permute-start
  69.1 4.5 %convolution_convert_fusion.1 = bf16[512,1024]{1,0:T(8,128)(2,1)S(1)} fusion(bf16[512,4096]{1,0:T(8,128)(2,1)S(1)} %copy-done.3, bf16[4096,1024]{1,0:T(8,128)(2,1)S(1)} %bitcast.48), kind=kOutput, calls=%fused_computation.14 | convolution fusion | flops 4295491584 | bytes 13631488 | tf_op jit(solution)/shard_map/dot_general | solution.py:25
  74.3 27.8 %collective-permute-done = bf16[2,4,128,256]{3,2,1,0:T(8,128)(2,1)} collective-permute-done((bf16[2,4,128,256]{3,2,1,0:T(8,128)(2,1)}, bf16[2,4,128,256]{3,2,1,0:T(8,128)(2,1)}, u32[]{:S(2)}, u32[]{:S(2)}) %collective-permute-start) | collective-permute-done | bytes 524320 | tf_op jit(solution)/shard_map/ppermute | solution.py:15
  102.2 1.9 collective-permute-start.4
  110.6 1.9 constant_dynamic-update-slice_fusion.6
  112.5 1.9 constant_dynamic-update-slice_fusion.5
  116.2 7.2 %collective-permute-done.4 = bf16[2,4,128,256]{3,2,1,0:T(8,128)(2,1)S(1)} collective-permute-done((bf16[2,4,128,256]{3,2,1,0:T(8,128)(2,1)}, bf16[2,4,128,256]{3,2,1,0:T(8,128)(2,1)S(1)}, u32[]{:S(2)}, u32[]{:S(2)}) %collective-permute-start.4) | collective-permute-done | bytes 524320 | tf_op jit(solution)/shard_map/ppermute | solution.py:15
  124.1 22.1 %collective-permute-done.5 = bf16[2,4,128,256]{3,2,1,0:T(8,128)(2,1)S(1)} collective-permute-done((bf16[2,4,128,256]{3,2,1,0:T(8,128)(2,1)}, bf16[2,4,128,256]{3,2,1,0:T(8,128)(2,1)S(1)}, u32[]{:S(2)}, u32[]{:S(2)}) %collective-permute-start.5) | collective-permute-done | bytes 524320 | tf_op jit(solution)/shard_map/ppermute | solution.py:15
  147.1 29.5 %collective-permute-done.6 = bf16[2,4,128,256]{3,2,1,0:T(8,128)(2,1)S(1)} collective-permute-done((bf16[2,4,128,256]{3,2,1,0:T(8,128)(2,1)}, bf16[2,4,128,256]{3,2,1,0:T(8,128)(2,1)S(1)}, u32[]{:S(2)}, u32[]{:S(2)}) %collective-permute-start.6) | collective-permute-done | bytes 524320 | tf_op jit(solution)/shard_map/ppermute | solution.py:15
  177.4 1.9 constant_dynamic-update-slice_fusion
  179.3 7.9 %gather_fusion = bf16[64,2,128,256]{3,2,1,0:T(8,128)(2,1)} fusion(bf16[2,36,128,256]{3,2,1,0:T(8,128)(2,1)} %constant_dynamic-update-slice_fusion, s32[1024]{0:T(1024)S(1)} %pad_clamp_fusion), kind=kCustom, calls=%fused_computation | custom fusion | bytes 16777472 | tf_op jit(solution)/shard_map/jit(_take)/gather | solution.py:42
  187.2 11.9 %copy.17 = bf16[64,2,128,256]{2,3,0,1:T(8,128)(2,1)} copy(bf16[64,2,128,256]{3,2,1,0:T(8,128)(2,1)} %gather_fusion) | data formatting | bytes 16777216 | tf_op jit(solution)/shard_map/jit(_take)/gather | solution.py:42
  199.1 5.2 %fusion.17 = (bf16[1,4,16,128,256]{3,4,2,1,0:T(8,128)(2,1)}, bf16[1,4,16,128,256]{3,4,2,1,0:T(8,128)(2,1)S(1)}) fusion(bf16[2,4,16,128,256]{3,4,2,1,0:T(8,128)(2,1)} %bitcast.39), kind=kLoop, calls=%fused_computation.40 | loop fusion | bytes 16777216 | tf_op jit(solution)/shard_map/slice | solution.py:46
  204.3 13.5 %fusion = (f32[4,2,4,128]{3,2,1,0:T(4,128)S(1)}, f32[4,2,16,128,128,4]{4,3,5,2,1,0:T(8,128)}) fusion(pred[4,128,16,128]{1,3,2,0:T(8,128)(4,1)S(1)} %or_and_fusion, bf16[4,128,2,4,128,1]{4,3,2,1,0,5:T(4,128)(2,1)S(1)} %bitcast.41, bf16[4,16,128,2,128,1]{2,4,3,1,0,5:T(8,128)(2,1)S(1)} %bitcast.40), kind=kOutput, calls=%fused_computation.4 | convolution fusion | flops 2172645376 | bytes 39862272 | tf_op jit(solution)/shard_map/bqhgd,bskhd->bhgqsk/dot_general | solution.py:63
  217.9 14.7 %fusion.1 = f32[4,2,4,128]{3,2,1,0:T(4,128)S(1)} fusion(f32[4,2,16,128,128,4]{4,3,5,2,1,0:T(8,128)} %get-tuple-element.10, f32[4,2,4,128]{3,2,1,0:T(4,128)S(1)} %get-tuple-element.9, pred[4,128,16,128]{1,3,2,0:T(8,128)(4,1)S(1)} %or_and_fusion), kind=kLoop, calls=%fused_computation.5 | loop fusion | flops 41938944 | bytes 34635776 | tf_op jit(solution)/shard_map/reduce_sum | solution.py:69
  232.6 16.9 %fusion.11 = bf16[4,128,2,4,128]{1,4,3,2,0:T(8,128)(2,1)S(1)} fusion(bf16[4,16,128,2,128,1]{2,4,3,1,0,5:T(8,128)(2,1)} %bitcast.42, f32[4,2,16,128,128,4]{4,3,5,2,1,0:T(8,128)} %get-tuple-element.10, f32[4,2,4,128]{3,2,1,0:T(4,128)S(1)} %fusion.1, f32[4,2,4,128]{3,2,1,0:T(4,128)S(1)} %get-tuple-element.9, pred[4,128,16,128]{1,3,2,0:T(8,128)(4,1)S(1)} %or_and_fusion), kind=kOutput, calls=%fused_computation.15 | convolution fusion | flops 2198339584 | bytes 39878656 | tf_op jit(solution)/shard_map/bhgqsk,bskhd->bqhgd/dot_general | solution.py:71
  251.0 9.5 %convolution_convert_fusion = bf16[512,4096]{1,0:T(8,128)(2,1)} fusion(bf16[512,1024]{1,0:T(8,128)(2,1)S(1)} %reshape.61, bf16[1024,4096]{1,0:T(8,128)(2,1)} %param.12), kind=kOutput, calls=%fused_computation.8 | convolution fusion | flops 4297064448 | bytes 13631488 | tf_op jit(solution)/shard_map/dot_general | solution.py:76
  260.6 42.1 %reduce-scatter.2.cloned.1.call-done = bf16[128,4096]{1,0:T(8,128)(2,1)} async-done(((bf16[512,4096]{1,0:T(8,128)(2,1)}), bf16[128,4096]{1,0:T(8,128)(2,1)}) %reduce-scatter.2.cloned.1.call-update) | async-done | bytes 1048592 | tf_op jit(solution)/shard_map/reduce_scatter | solution.py:75
  (46 shorter events, 21.8 us)
Async XLA Ops:
  6.5 37.2 %copy-start = (bf16[4096,256]{1,0:T(8,128)(2,1)S(1)}, bf16[4096,256]{1,0:T(8,128)(2,1)}, u32[]{:S(2)}) copy-start(bf16[4096,256]{1,0:T(8,128)(2,1)} %param.11) | copy-start | bytes 6291460
  6.5 37.2 %all-gather.2.cloned.1.call-start = ((), (), s32[]{:S(2)}) async-start(), calls=%async_computation.1 | async-start | bytes 5242880 | tf_op jit(solution)/shard_map/all_gather | solution.py:22
  7.3 295.4 %reduce-scatter.2.cloned.1.call-start = ((), (), s32[]{:S(2)}) async-start(), calls=%async_computation.2 | async-start | bytes 5242880 | tf_op jit(solution)/shard_map/reduce_scatter | solution.py:75
  43.7 3.6 %copy-start.4 = (bf16[4096,256]{1,0:T(8,128)(2,1)S(1)}, bf16[4096,256]{1,0:T(8,128)(2,1)}, u32[]{:S(2)}) copy-start(bf16[4096,256]{1,0:T(8,128)(2,1)} %param.10) | copy-start | bytes 6291460
  43.7 25.4 %slice-start = ((s8[8388608]{0:T(1024)(128)(4,1)}), s8[4194304]{0:T(1024)(128)(4,1)S(1)}, s32[]{:S(2)}) async-start(s8[8388608]{0:T(1024)(128)(4,1)} %bitcast.47), calls=%async_computation.3 | async-start | bytes 8388608
  47.3 21.8 %slice-start.1 = ((s8[8388608]{0:T(1024)(128)(4,1)}), s8[4194304]{0:T(1024)(128)(4,1)S(1)}, s32[]{:S(2)}) async-start(s8[8388608]{0:T(1024)(128)(4,1)} %bitcast.47), calls=%async_computation.4 | async-start | bytes 8388608
  47.3 21.7 %copy-start.3 = (bf16[512,4096]{1,0:T(8,128)(2,1)S(1)}, bf16[512,4096]{1,0:T(8,128)(2,1)}, u32[]{:S(2)}) copy-start(bf16[512,4096]{1,0:T(8,128)(2,1)} %all-gather.2.cloned.1.call-done) | copy-start | bytes 12582916
  50.9 18.1 %copy-start.2 = (bf16[512,256]{1,0:T(8,128)(2,1)}, bf16[512,256]{1,0:T(8,128)(2,1)S(1)}, u32[]{:S(2)}) copy-start(bf16[512,256]{1,0:T(8,128)(2,1)S(1)} %convolution_convert_fusion.3) | copy-start | bytes 786436
  51.9 125.6 %collective-permute-start.7 = (bf16[2,4,128,256]{3,2,1,0:T(8,128)(2,1)}, bf16[2,4,128,256]{3,2,1,0:T(8,128)(2,1)}, u32[]{:S(2)}, u32[]{:S(2)}) collective-permute-start(bf16[2,4,128,256]{3,2,1,0:T(8,128)(2,1)} %pad_maximum_fusion), channel_id=1, source_target_pairs={{16,0},{20,4},{24,8},{28,12},{17,1},{21,5},{25,9},{29,13},{18,2},{... | collective-permute-start | bytes 1572872 | tf_op jit(solution)/shard_map/ppermute | solution.py:15
  53.1 59.3 %collective-permute-start.3 = (bf16[2,4,128,256]{3,2,1,0:T(8,128)(2,1)}, bf16[2,4,128,256]{3,2,1,0:T(8,128)(2,1)}, u32[]{:S(2)}, u32[]{:S(2)}) collective-permute-start(bf16[2,4,128,256]{3,2,1,0:T(8,128)(2,1)} %pad_maximum_fusion), channel_id=1, source_target_pairs={{0,4},{4,8},{8,12},{12,16},{16,20},{20,24},{24,28},{1,5},{5,9},{9,... | collective-permute-start | bytes 1572872 | tf_op jit(solution)/shard_map/ppermute | solution.py:15
  56.5 52.6 %collective-permute-start.2 = (bf16[2,4,128,256]{3,2,1,0:T(8,128)(2,1)}, bf16[2,4,128,256]{3,2,1,0:T(8,128)(2,1)}, u32[]{:S(2)}, u32[]{:S(2)}) collective-permute-start(bf16[2,4,128,256]{3,2,1,0:T(8,128)(2,1)} %pad_maximum_fusion), channel_id=1, source_target_pairs={{0,8},{4,12},{8,16},{12,20},{16,24},{20,28},{1,9},{5,13},{9,17},{1... | collective-permute-start | bytes 1572872 | tf_op jit(solution)/shard_map/ppermute | solution.py:15
  62.4 43.5 %collective-permute-start.1 = (bf16[2,4,128,256]{3,2,1,0:T(8,128)(2,1)}, bf16[2,4,128,256]{3,2,1,0:T(8,128)(2,1)}, u32[]{:S(2)}, u32[]{:S(2)}) collective-permute-start(bf16[2,4,128,256]{3,2,1,0:T(8,128)(2,1)} %pad_maximum_fusion), channel_id=1, source_target_pairs={{0,12},{4,16},{8,20},{12,24},{16,28},{1,13},{5,17},{9,21},{13,25},... | collective-permute-start | bytes 1572872 | tf_op jit(solution)/shard_map/ppermute | solution.py:15
  66.9 35.2 %collective-permute-start = (bf16[2,4,128,256]{3,2,1,0:T(8,128)(2,1)}, bf16[2,4,128,256]{3,2,1,0:T(8,128)(2,1)}, u32[]{:S(2)}, u32[]{:S(2)}) collective-permute-start(bf16[2,4,128,256]{3,2,1,0:T(8,128)(2,1)} %pad_maximum_fusion), channel_id=1, source_target_pairs={{0,16},{4,20},{8,24},{12,28},{1,17},{5,21},{9,25},{13,29},{2,18},{... | collective-permute-start | bytes 1572872 | tf_op jit(solution)/shard_map/ppermute | solution.py:15
  102.2 21.1 %collective-permute-start.4 = (bf16[2,4,128,256]{3,2,1,0:T(8,128)(2,1)}, bf16[2,4,128,256]{3,2,1,0:T(8,128)(2,1)S(1)}, u32[]{:S(2)}, u32[]{:S(2)}) collective-permute-start(bf16[2,4,128,256]{3,2,1,0:T(8,128)(2,1)} %pad_maximum_fusion), channel_id=1, source_target_pairs={{4,0},{8,4},{12,8},{16,12},{20,16},{24,20},{28,24},{5,1},{9,5},{13... | collective-permute-start | bytes 1572872 | tf_op jit(solution)/shard_map/ppermute | solution.py:15
  106.0 40.3 %collective-permute-start.5 = (bf16[2,4,128,256]{3,2,1,0:T(8,128)(2,1)}, bf16[2,4,128,256]{3,2,1,0:T(8,128)(2,1)S(1)}, u32[]{:S(2)}, u32[]{:S(2)}) collective-permute-start(bf16[2,4,128,256]{3,2,1,0:T(8,128)(2,1)} %pad_maximum_fusion), channel_id=1, source_target_pairs={{8,0},{12,4},{16,8},{20,12},{24,16},{28,20},{9,1},{13,5},{17,9},{2... | collective-permute-start | bytes 1572872 | tf_op jit(solution)/shard_map/ppermute | solution.py:15
  109.1 67.4 %collective-permute-start.6 = (bf16[2,4,128,256]{3,2,1,0:T(8,128)(2,1)}, bf16[2,4,128,256]{3,2,1,0:T(8,128)(2,1)S(1)}, u32[]{:S(2)}, u32[]{:S(2)}) collective-permute-start(bf16[2,4,128,256]{3,2,1,0:T(8,128)(2,1)} %pad_maximum_fusion), channel_id=1, source_target_pairs={{12,0},{16,4},{20,8},{24,12},{28,16},{13,1},{17,5},{21,9},{25,13},... | collective-permute-start | bytes 1572872 | tf_op jit(solution)/shard_map/ppermute | solution.py:15
  251.0 51.7 %copy-start.1 = (bf16[4096,256]{1,0:T(8,128)(2,1)S(1)}, bf16[4096,256]{1,0:T(8,128)(2,1)}, u32[]{:S(2)}) copy-start(bf16[4096,256]{1,0:T(8,128)(2,1)} %param.11) | copy-start | bytes 6291460
Sparse Core Ops, SparseCore 0:
  8.9 34.7 all-gather.1
  260.7 41.9 reduce-scatter.1
where the time goes:
time: 313 us; the launch traced here: 310 us
  waiting for transfers between devices  160 us (51%)
  matrix products  51.6 us (16%)
  local copies, waits for them, and re-layouts  39.3 us (13%)
  other arithmetic  23.1 us (7%)
  starting transfers between devices  21.9 us (7%)
  between operations  13.6 us (4%)
    ppermute x8, waiting for transfers between devices, from_behind(): return lax.ppermute(block, axis, route)  86.6 us
    reduce_scatter x1, waiting for transfers between devices, local(): lax.psum_scatter(jnp.dot(attended, out_weight, preferred_element_type=jnp...  42.1 us
    all_gather x1, waiting for transfers between devices, local(): piece = lax.all_gather(tokens, 'tp', axis=1, tiled=True)  30.6 us
    ppermute x8, starting transfers between devices, from_behind(): return lax.ppermute(block, axis, route)  21.8 us
    gather x2, local copies, waits for them, and re-layouts, local(): chosen = jnp.take(source, links - anchor, axis=1, mode='clip')  19.8 us
    dot_general x1, matrix products, local(): jnp.einsum('bhgqsk,bskhd->bqhgd', weights, chosen_values, preferred_eleme...  16.9 us
    reduce_sum x1, other arithmetic, local(): total = jnp.sum(powers, axis=(4, 5), keepdims=True)  14.7 us
    dot_general x1, matrix products, local(): jnp.einsum('bqhgd,bskhd->bhgqsk', query_blocks, chosen_keys, preferred_el...  13.5 us
  transfers between devices with their start and end apart: 10, of which 6 were waited for; matrix products, arithmetic and copies ran while one was open for 7% of the time, Pallas kernels for 0%

commit v1 on v0

v1 whole, which is shorter than its diff:
```python
import functools

import jax
import jax.numpy as jnp
from jax import lax
from jax.experimental import pallas as pl
from jax.experimental.pallas import tpu as pltpu
from jax.sharding import PartitionSpec as P

HEAD_DIM = 128
BLOCK = 128
LINKS = 16
REACH = 4
CORES = 2
BF16 = jnp.bfloat16
F32 = jnp.float32
VMEM = pl.BlockSpec(memory_space=pltpu.VMEM)
SMEM = pl.BlockSpec(memory_space=pltpu.SMEM)
ANY = pl.BlockSpec(memory_space=pl.ANY)
GRANT = 56 * 1024 * 1024


def attend_kernel(
    blocks, kv_heads, group, place_ref, links_ref, counts_ref, docs_ref, query_ref, source_ref,
    out_ref, key_buf, value_buf, score_buf, sum_buf, acc_buf, live_ref, sems
):
    first, anchor = place_ref[0], place_ref[1]

    def copies(block, position, listed):
        at = listed - anchor
        rows = pl.ds(pl.multiple_of(position * BLOCK, BLOCK), BLOCK)
        return (
            pltpu.make_async_copy(
                source_ref.at[at, 0], key_buf.at[block, rows], sems.at[block, position, 0]
            ),
            pltpu.make_async_copy(
                source_ref.at[at, 1], value_buf.at[block, rows], sems.at[block, position, 1]
            ),
        )

    for block in range(blocks):
        mine = first + block
        doc = docs_ref[mine]

        def pick(slot, position, block=block, mine=mine, doc=doc):
            listed = links_ref[block, slot]
            seen = (slot < counts_ref[block]) & (
                (listed <= mine) | (docs_ref[listed] != doc)
            )

            @pl.when(seen)
            def _():
                for copy in copies(block, position, listed):
                    copy.start()

            return position + seen.astype(jnp.int32)

        live = lax.fori_loop(0, LINKS, pick, jnp.int32(0))
        live_ref[block] = live

        @pl.when(lax.rem(live, 2) == 1)
        def _(block=block, mine=mine, live=live):
            for copy in copies(block, live, mine):
                copy.start()

    scale = HEAD_DIM ** (-0.5) * 1.4426950408889634
    pair = 2 * BLOCK
    height = group * BLOCK
    token = lax.rem(lax.broadcasted_iota(jnp.int32, (height, pair), 0), BLOCK)
    column = lax.broadcasted_iota(jnp.int32, (height, pair), 1)
    row_column = lax.broadcasted_iota(jnp.int32, (1, pair), 1)

    def one(block, carry):
        live = live_ref[block]
        pairs = lax.div(live + 1, 2)

        def land(position, carry):
            for copy in copies(block, position, anchor):
                copy.wait()
            return carry

        lax.fori_loop(0, pairs * 2, land, 0)
        rows = pl.ds(pl.multiple_of(block * BLOCK, BLOCK), BLOCK)
        for head in range(kv_heads):
            lanes = pl.ds(head * HEAD_DIM, HEAD_DIM)
            query = jnp.concatenate(
                [
                    query_ref[rows, pl.ds((head * group + member) * HEAD_DIM, HEAD_DIM)]
                    for member in range(group)
                ],
                axis=0,
            )

            def scores_of(index):
                keys = key_buf[block, pl.ds(pl.multiple_of(index * pair, pair), pair), lanes]
                scores = lax.dot_general(
                    query, keys, (((1,), (1,)), ((), ())), preferred_element_type=F32
                )
                bound = (live - index * 2) * BLOCK
                return scores * scale + jnp.where(row_column < bound, 0.0, -1e30)

            def halves_max(scores):
                return jnp.maximum(scores[:, :BLOCK], scores[:, BLOCK:])

            scores = scores_of(0)
            scores = jnp.where((column >= BLOCK) | (column <= token), scores, -1e30)
            score_buf[0] = scores

            def first_pass(index, top):
                scores = scores_of(index)
                score_buf[index] = scores
                return jnp.maximum(top, halves_max(scores))

            top = lax.fori_loop(1, pairs, first_pass, halves_max(scores))
            top = jnp.max(top, axis=1, keepdims=True)
            acc_buf[...] = jnp.zeros_like(acc_buf)
            sum_buf[...] = jnp.zeros_like(sum_buf)

            def second_pass(index, carry):
                powers = jnp.exp2(score_buf[index] - top)
                sum_buf[...] += powers[:, :BLOCK] + powers[:, BLOCK:]
                values = value_buf[block, pl.ds(pl.multiple_of(index * pair, pair), pair), lanes]
                acc_buf[...] += jnp.dot(
                    powers.astype(BF16), values, preferred_element_type=F32
                )
                return carry

            lax.fori_loop(0, pairs, second_pass, 0)
            total = jnp.sum(sum_buf[...], axis=1, keepdims=True)
            result = (acc_buf[...] / total).astype(BF16)
            for member in range(group):
                out_ref[rows, pl.ds((head * group + member) * HEAD_DIM, HEAD_DIM)] = result[
                    member * BLOCK : (member + 1) * BLOCK
                ]
        return carry

    lax.fori_loop(0, blocks, one, 0)


def attend(place, links, counts, doc_ids, query, source):
    row_count, query_width = query.shape
    key_width = source.shape[3]
    blocks = row_count // BLOCK
    kv_heads = key_width // HEAD_DIM
    group = query_width // key_width
    keys = LINKS * BLOCK
    height = group * BLOCK
    return pl.pallas_call(
        functools.partial(attend_kernel, blocks, kv_heads, group),
        out_shape=jax.ShapeDtypeStruct(query.shape, BF16),
        in_specs=[SMEM] * 4 + [VMEM, ANY],
        out_specs=VMEM,
        scratch_shapes=[
            pltpu.VMEM((blocks, keys, key_width), BF16),
            pltpu.VMEM((blocks, keys, key_width), BF16),
            pltpu.VMEM((LINKS // 2, height, 2 * BLOCK), F32),
            pltpu.VMEM((height, BLOCK), F32),
            pltpu.VMEM((height, HEAD_DIM), F32),
            pltpu.SMEM((blocks,), jnp.int32),
            pltpu.SemaphoreType.DMA((blocks, LINKS, 2)),
        ],
        compiler_params=pltpu.CompilerParams(vmem_limit_bytes=GRANT),
        cost_estimate=pl.CostEstimate(
            flops=4 * row_count * query_width * keys, bytes_accessed=1 << 23, transcendentals=0
        ),
    )(place, links, counts, doc_ids, query, source)


def project_kernel(
    tp, chunks, wide, attended_ref, weight_ref, out_ref, weight_buf, part_buf, own_buf,
    mate_send, mate_recv, far_send, far_recv, weight_sems, mate_send_sems, mate_recv_sems,
    far_send_sems, far_recv_sems
):
    rows = attended_ref.shape[0] // tp
    across = tp // CORES
    me = lax.axis_index("tp")
    chip, core = lax.div(me, CORES), lax.rem(me, CORES)
    mate = chip * CORES + 1 - core

    def weight_copy(index):
        columns = pl.ds(pl.multiple_of(index * wide, wide), wide)
        return pltpu.make_async_copy(
            weight_ref.at[:, columns], weight_buf.at[index], weight_sems.at[index]
        )

    def start_weight(index, carry):
        weight_copy(index).start()
        return carry

    lax.fori_loop(0, chunks, start_weight, 0)

    barrier = pltpu.get_barrier_semaphore()
    pl.semaphore_signal(barrier, inc=1, device_id={"tp": mate})
    for step in range(1, across):
        other = lax.rem(chip + step, across) * CORES + core
        pl.semaphore_signal(barrier, inc=1, device_id={"tp": other})
    pl.semaphore_wait(barrier, across)

    def mate_copy(index):
        return pltpu.make_async_remote_copy(
            src_ref=mate_send.at[index],
            dst_ref=mate_recv.at[index],
            send_sem=mate_send_sems.at[index],
            recv_sem=mate_recv_sems.at[index],
            device_id={"tp": mate},
        )

    def far_copy(index, step):
        other = lax.rem(chip + step, across) * CORES + core
        return pltpu.make_async_remote_copy(
            src_ref=far_send.at[index, step - 1],
            dst_ref=far_recv.at[index, step - 1],
            send_sem=far_send_sems.at[index, step - 1],
            recv_sem=far_recv_sems.at[index, step - 1],
            device_id={"tp": other},
        )

    def rows_of(step, which):
        start = (lax.rem(chip + step, across) * CORES + which) * rows
        return pl.ds(pl.multiple_of(start, rows), rows)

    def multiply(index):
        weight_copy(index).wait()
        part_buf[lax.rem(index, 2)] = jnp.dot(
            attended_ref[...], weight_buf[index], preferred_element_type=F32
        )
        for step in range(across):
            mate_send[index, step] = part_buf[
                lax.rem(index, 2), rows_of(step, 1 - core)
            ].astype(BF16)
        mate_copy(index).start()

    def combine(index):
        mate_copy(index).wait_recv()
        for step in range(across):
            total = part_buf[lax.rem(index, 2), rows_of(step, core)] + mate_recv[
                index, step
            ].astype(F32)
            if step == 0:
                own_buf[index] = total
            else:
                far_send[index, step - 1] = total.astype(BF16)
                far_copy(index, step).start()

    multiply(0)

    def middle(index, carry):
        multiply(index)
        combine(index - 1)
        return carry

    lax.fori_loop(1, chunks, middle, 0)
    combine(chunks - 1)

    def finish(index, carry):
        total = own_buf[index]
        for step in range(1, across):
            far_copy(index, step).wait_recv()
            total = total + far_recv[index, step - 1].astype(F32)
        columns = pl.ds(pl.multiple_of(index * wide, wide), wide)
        out_ref[:, columns] = total.astype(BF16)
        return carry

    lax.fori_loop(0, chunks, finish, 0)

    def drain(index, carry):
        mate_copy(index).wait_send()
        for step in range(1, across):
            far_copy(index, step).wait_send()
        return carry

    lax.fori_loop(0, chunks, drain, 0)


def project(attended, out_weight):
    tp = lax.axis_size("tp")
    across = tp // CORES
    row_count, depth = attended.shape
    width = out_weight.shape[1]
    rows = row_count // tp
    wide = min(512, width)
    chunks = width // wide
    return pl.pallas_call(
        functools.partial(project_kernel, tp, chunks, wide),
        out_shape=jax.ShapeDtypeStruct((rows, width), BF16),
        in_specs=[VMEM, ANY],
        out_specs=VMEM,
        scratch_shapes=[
            pltpu.VMEM((chunks, depth, wide), BF16),
            pltpu.VMEM((2, row_count, wide), F32),
            pltpu.VMEM((chunks, rows, wide), F32),
            pltpu.VMEM((chunks, across, rows, wide), BF16),
            pltpu.VMEM((chunks, across, rows, wide), BF16),
            pltpu.VMEM((chunks, across - 1, rows, wide), BF16),
            pltpu.VMEM((chunks, across - 1, rows, wide), BF16),
            pltpu.SemaphoreType.DMA((chunks,)),
            pltpu.SemaphoreType.DMA((chunks,)),
            pltpu.SemaphoreType.DMA((chunks,)),
            pltpu.SemaphoreType.DMA((chunks, across - 1)),
            pltpu.SemaphoreType.DMA((chunks, across - 1)),
        ],
        compiler_params=pltpu.CompilerParams(
            collective_id=1, has_side_effects=True, vmem_limit_bytes=GRANT
        ),
        cost_estimate=pl.CostEstimate(
            flops=2 * row_count * depth * width, bytes_accessed=1 << 24, transcendentals=0
        ),
    )(attended, out_weight)


def from_behind(block, axis, distance):
    devices = range(lax.axis_size(axis))
    route = [(i - distance, i) for i in devices if i - distance in devices]
    return lax.ppermute(block, axis, route)


def local(tokens, query_weight, key_weight, value_weight, out_weight, links, counts, doc_ids):
    row_count = tokens.shape[0]
    key_width = key_weight.shape[1]
    piece = lax.all_gather(tokens, "tp", axis=1, tiled=True)
    weights = (query_weight, key_weight, value_weight)
    query, keys, values = tuple(
        jnp.dot(piece, weight, preferred_element_type=F32).astype(BF16) for weight in weights
    )
    block_count = row_count // BLOCK
    stacked = jnp.stack(
        [keys.reshape(block_count, BLOCK, key_width), values.reshape(block_count, BLOCK, key_width)],
        axis=1,
    )
    position = lax.axis_index("ctx")
    pieces = []
    for offset in range(-REACH, REACH + 1):
        if offset == 0:
            pieces.append(stacked)
        else:
            pieces.append(from_behind(stacked, "ctx", -offset))
    source = jnp.concatenate(pieces, axis=0)
    place = jnp.stack([position * block_count, (position - REACH) * block_count]).astype(jnp.int32)
    attended = attend(place, links, counts, doc_ids, query, source)
    return project(attended, out_weight)


def solution(mesh):
    placed = (
        P("ctx", "tp"),
        P(None, "tp"),
        P(None, "tp"),
        P(None, "tp"),
        P("tp", None),
        P("ctx", None),
        P("ctx"),
        P(),
    )
    return jax.shard_map(
        local, mesh=mesh, in_specs=placed, out_specs=P(("ctx", "tp"), None), check_vma=False
    )
```

time: 313 us -> 213 us (0.68)
  the two profiles are of different devices: /device:TPU:6 before, /device:TPU:0 now
where the time goes in v1:
time: 213 us; the launch traced here: 212 us
  waiting for transfers between devices  108 us (51%)
  Pallas kernels  54.9 us (26%)
  starting transfers between devices  18.2 us (9%)
  between operations  13.7 us (6%)
  matrix products  12.6 us (6%)
  local copies, waits for them, and re-layouts  4.71 us (2%)
    ppermute x8, waiting for transfers between devices, from_behind(): return lax.ppermute(block, axis, route)  68.7 us
    all_gather x1, waiting for transfers between devices, local(): piece = lax.all_gather(tokens, 'tp', axis=1, tiled=True)  38.2 us
    pallas_call x1, Pallas kernels, project(): pl.pallas_call(functools.partial(project_kernel, tp, chunks, wide), out_s...  30.1 us
    pallas_call x1, Pallas kernels, attend(): pl.pallas_call(functools.partial(attend_kernel, blocks, kv_heads, group),...  24.7 us
    ppermute x8, starting transfers between devices, from_behind(): return lax.ppermute(block, axis, route)  18.2 us
    dot_general x3, matrix products, local(): jnp.dot(piece, weight, preferred_element_type=F32).astype(BF16)  12.6 us
    unnamed x20, local copies, waits for them, and re-layouts  4.68 us
  transfers between devices with their start and end apart: 9, of which 5 were waited for; matrix products, arithmetic and copies ran while one was open for 3% of the time, Pallas kernels for 0%

profile of v1, /device:TPU:0, one launch (start us, length us, event | category | flops | bytes accessed | tf_op | source)
XLA Modules:
  0.0 212.5 jit_solution(7946966100246095077)
XLA Ops:
  6.5 0.7 all-gather.2.cloned.1.call-update
  7.3 0.7 pad_add_fusion.place_ref
  7.9 38.2 %all-gather.2.cloned.1.call-done = bf16[512,4096]{1,0:T(8,128)(2,1)} async-done(((bf16[512,1024]{1,0:T(8,128)(2,1)}), bf16[512,4096]{1,0:T(8,128)(2,1)}) %all-gather.2.cloned.1.call-update) | async-done | bytes 4194320 | tf_op jit(solution)/shard_map/all_gather | solution.py:320
  46.1 3.6 %convolution_convert_fusion.1 = bf16[512,256]{1,0:T(8,128)(2,1)S(1)} fusion(bf16[512,4096]{1,0:T(8,128)(2,1)} %all-gather.2.cloned.1.call-done, bf16[4096,256]{1,0:T(8,128)(2,1)S(1)} %copy-done), kind=kOutput, calls=%fused_computation.1 | convolution fusion | flops 1073872896 | bytes 6553600 | tf_op jit(solution)/shard_map/dot_general | solution.py:323
  49.7 0.0 slice-start.1
  49.8 3.6 %convolution_convert_fusion.2 = bf16[512,256]{1,0:T(8,128)(2,1)S(1)} fusion(bf16[512,4096]{1,0:T(8,128)(2,1)} %all-gather.2.cloned.1.call-done, bf16[4096,256]{1,0:T(8,128)(2,1)S(1)} %copy-done.3), kind=kOutput, calls=%fused_computation.2 | convolution fusion | flops 1073872896 | bytes 6553600 | tf_op jit(solution)/shard_map/dot_general | solution.py:323
  53.4 0.1 pad_maximum_fusion
  53.4 4.3 %collective-permute-start = (bf16[4,2,128,256]{3,2,1,0:T(8,128)(2,1)S(1)}, bf16[4,2,128,256]{3,2,1,0:T(8,128)(2,1)S(1)}, u32[]{:S(2)}, u32[]{:S(2)}) collective-permute-start(bf16[4,2,128,256]{3,2,1,0:T(8,128)(2,1)S(1)} %pad_maximum_fusion), channel_id=1, source_target_pairs={{0,16},{4,20},{8,24},{12,28},{1,17},{5,21},{9,25},{13,29},{2,18},{... | collective-permute-start | bytes 1572872 | tf_op jit(solution)/shard_map/ppermute | solution.py:314
  57.8 4.3 %collective-permute-start.1 = (bf16[4,2,128,256]{3,2,1,0:T(8,128)(2,1)S(1)}, bf16[4,2,128,256]{3,2,1,0:T(8,128)(2,1)S(1)}, u32[]{:S(2)}, u32[]{:S(2)}) collective-permute-start(bf16[4,2,128,256]{3,2,1,0:T(8,128)(2,1)S(1)} %pad_maximum_fusion), channel_id=1, source_target_pairs={{0,12},{4,16},{8,20},{12,24},{16,28},{1,13},{5,17},{9,21},{13,25},... | collective-permute-start | bytes 1572872 | tf_op jit(solution)/shard_map/ppermute | solution.py:314
  62.1 1.3 collective-permute-start.2
  63.5 3.1 %collective-permute-start.3 = (bf16[4,2,128,256]{3,2,1,0:T(8,128)(2,1)S(1)}, bf16[4,2,128,256]{3,2,1,0:T(8,128)(2,1)S(1)}, u32[]{:S(2)}, u32[]{:S(2)}) collective-permute-start(bf16[4,2,128,256]{3,2,1,0:T(8,128)(2,1)S(1)} %pad_maximum_fusion), channel_id=1, source_target_pairs={{0,4},{4,8},{8,12},{12,16},{16,20},{20,24},{24,28},{1,5},{5,9},{9,... | collective-permute-start | bytes 1572872 | tf_op jit(solution)/shard_map/ppermute | solution.py:314
  66.6 1.3 collective-permute-start.4
  67.9 5.5 %convolution_convert_fusion.query_ref = bf16[512,1024]{1,0:T(8,128)(2,1)} fusion(bf16[512,4096]{1,0:T(8,128)(2,1)S(1)} %copy-done.2, bf16[4096,1024]{1,0:T(8,128)(2,1)S(1)} %bitcast.15), kind=kOutput, calls=%fused_computation | convolution fusion | flops 4295491584 | bytes 13631488 | tf_op jit(solution)/shard_map/dot_general | solution.py:323
  73.4 1.3 collective-permute-start.5
  74.7 16.0 %collective-permute-done.1 = bf16[4,2,128,256]{3,2,1,0:T(8,128)(2,1)S(1)} collective-permute-done((bf16[4,2,128,256]{3,2,1,0:T(8,128)(2,1)S(1)}, bf16[4,2,128,256]{3,2,1,0:T(8,128)(2,1)S(1)}, u32[]{:S(2)}, u32[]{:S(2)}) %collective-permute-start.1) | collective-permute-done | bytes 524320 | tf_op jit(solution)/shard_map/ppermute | solution.py:314
  90.7 1.3 collective-permute-start.6
  92.0 9.2 %collective-permute-done.2 = bf16[4,2,128,256]{3,2,1,0:T(8,128)(2,1)S(1)} collective-permute-done((bf16[4,2,128,256]{3,2,1,0:T(8,128)(2,1)S(1)}, bf16[4,2,128,256]{3,2,1,0:T(8,128)(2,1)S(1)}, u32[]{:S(2)}, u32[]{:S(2)}) %collective-permute-start.2) | collective-permute-done | bytes 524320 | tf_op jit(solution)/shard_map/ppermute | solution.py:314
  101.2 1.3 collective-permute-start.7
  102.8 16.7 %collective-permute-done.6 = bf16[4,2,128,256]{3,2,1,0:T(8,128)(2,1)S(1)} collective-permute-done((bf16[4,2,128,256]{3,2,1,0:T(8,128)(2,1)S(1)}, bf16[4,2,128,256]{3,2,1,0:T(8,128)(2,1)S(1)}, u32[]{:S(2)}, u32[]{:S(2)}) %collective-permute-start.6) | collective-permute-done | bytes 524320 | tf_op jit(solution)/shard_map/ppermute | solution.py:314
  119.5 26.8 %collective-permute-done.7 = bf16[4,2,128,256]{3,2,1,0:T(8,128)(2,1)S(1)} collective-permute-done((bf16[4,2,128,256]{3,2,1,0:T(8,128)(2,1)S(1)}, bf16[4,2,128,256]{3,2,1,0:T(8,128)(2,1)S(1)}, u32[]{:S(2)}, u32[]{:S(2)}) %collective-permute-start.7) | collective-permute-done | bytes 524320 | tf_op jit(solution)/shard_map/ppermute | solution.py:314
  146.3 2.1 copy-done.1
  148.4 24.7 %shard_map.82.attended_ref = bf16[512,1024]{1,0:T(8,128)(2,1)} custom-call(s32[2]{0:T(128)} %pad_add_fusion.place_ref, s32[4,16]{1,0:T(4,128)} %links_ref.1, s32[4]{0:T(128)} %counts_ref.1, s32[32]{0:T(128)} %docs_ref.1, bf16[512,1024]{1,0:T(8,128)(2,1)} %convolution_convert_fusion.query_ref, bf16[36,2,128,256]{3,2,1,0:T(8,128)(2,1)} %copy-done.1), custom_call_target="tpu_custom_call" | custom-call | flops 4294967296 | bytes 8388608 | tf_op jit(solution)/shard_map/pallas_call | solution.py:148
  173.2 30.1 %shard_map.83 = bf16[128,4096]{1,0:T(8,128)(2,1)} custom-call(bf16[512,1024]{1,0:T(8,128)(2,1)} %shard_map.82.attended_ref, bf16[1024,4096]{1,0:T(8,128)(2,1)} %weight_ref.1), custom_call_target="tpu_custom_call" | custom-call | flops 4294967296 | bytes 16777216 | tf_op jit(solution)/shard_map/pallas_call | solution.py:283
  203.3 2.3 %copy.18 = bf16[128,4096]{1,0:T(8,128)(2,1)} copy(bf16[128,4096]{1,0:T(8,128)(2,1)} %shard_map.83) | data formatting | bytes 2097152
  (25 shorter events, 0.4 us)
Async XLA Ops:
  6.5 39.6 %copy-start = (bf16[4096,256]{1,0:T(8,128)(2,1)S(1)}, bf16[4096,256]{1,0:T(8,128)(2,1)}, u32[]{:S(2)}) copy-start(bf16[4096,256]{1,0:T(8,128)(2,1)} %param.11) | copy-start | bytes 6291460
  6.5 39.6 %all-gather.2.cloned.1.call-start = ((), (), s32[]{:S(2)}) async-start(), calls=%async_computation | async-start | bytes 5242880 | tf_op jit(solution)/shard_map/all_gather | solution.py:320
  46.1 3.6 %copy-start.3 = (bf16[4096,256]{1,0:T(8,128)(2,1)S(1)}, bf16[4096,256]{1,0:T(8,128)(2,1)}, u32[]{:S(2)}) copy-start(bf16[4096,256]{1,0:T(8,128)(2,1)} %param.10) | copy-start | bytes 6291460
  46.1 21.7 %slice-start = ((s8[8388608]{0:T(1024)(128)(4,1)}), s8[4194304]{0:T(1024)(128)(4,1)S(1)}, s32[]{:S(2)}) async-start(s8[8388608]{0:T(1024)(128)(4,1)} %bitcast.14), calls=%async_computation.1 | async-start | bytes 8388608
  49.7 18.1 %slice-start.1 = ((s8[8388608]{0:T(1024)(128)(4,1)}), s8[4194304]{0:T(1024)(128)(4,1)S(1)}, s32[]{:S(2)}) async-start(s8[8388608]{0:T(1024)(128)(4,1)} %bitcast.14), calls=%async_computation.2 | async-start | bytes 8388608
  49.8 18.1 %copy-start.2 = (bf16[512,4096]{1,0:T(8,128)(2,1)S(1)}, bf16[512,4096]{1,0:T(8,128)(2,1)}, u32[]{:S(2)}) copy-start(bf16[512,4096]{1,0:T(8,128)(2,1)} %all-gather.2.cloned.1.call-done) | copy-start | bytes 12582916
  53.4 19.9 %collective-permute-start = (bf16[4,2,128,256]{3,2,1,0:T(8,128)(2,1)S(1)}, bf16[4,2,128,256]{3,2,1,0:T(8,128)(2,1)S(1)}, u32[]{:S(2)}, u32[]{:S(2)}) collective-permute-start(bf16[4,2,128,256]{3,2,1,0:T(8,128)(2,1)S(1)} %pad_maximum_fusion), channel_id=1, source_target_pairs={{0,16},{4,20},{8,24},{12,28},{1,17},{5,21},{9,25},{13,29},{2,18},{... | collective-permute-start | bytes 1572872 | tf_op jit(solution)/shard_map/ppermute | solution.py:314
  57.8 32.9 %collective-permute-start.1 = (bf16[4,2,128,256]{3,2,1,0:T(8,128)(2,1)S(1)}, bf16[4,2,128,256]{3,2,1,0:T(8,128)(2,1)S(1)}, u32[]{:S(2)}, u32[]{:S(2)}) collective-permute-start(bf16[4,2,128,256]{3,2,1,0:T(8,128)(2,1)S(1)} %pad_maximum_fusion), channel_id=1, source_target_pairs={{0,12},{4,16},{8,20},{12,24},{16,28},{1,13},{5,17},{9,21},{13,25},... | collective-permute-start | bytes 1572872 | tf_op jit(solution)/shard_map/ppermute | solution.py:314
  62.1 39.1 %collective-permute-start.2 = (bf16[4,2,128,256]{3,2,1,0:T(8,128)(2,1)S(1)}, bf16[4,2,128,256]{3,2,1,0:T(8,128)(2,1)S(1)}, u32[]{:S(2)}, u32[]{:S(2)}) collective-permute-start(bf16[4,2,128,256]{3,2,1,0:T(8,128)(2,1)S(1)} %pad_maximum_fusion), channel_id=1, source_target_pairs={{0,8},{4,12},{8,16},{12,20},{16,24},{20,28},{1,9},{5,13},{9,17},{1... | collective-permute-start | bytes 1572872 | tf_op jit(solution)/shard_map/ppermute | solution.py:314
  63.5 39.1 %collective-permute-start.3 = (bf16[4,2,128,256]{3,2,1,0:T(8,128)(2,1)S(1)}, bf16[4,2,128,256]{3,2,1,0:T(8,128)(2,1)S(1)}, u32[]{:S(2)}, u32[]{:S(2)}) collective-permute-start(bf16[4,2,128,256]{3,2,1,0:T(8,128)(2,1)S(1)} %pad_maximum_fusion), channel_id=1, source_target_pairs={{0,4},{4,8},{8,12},{12,16},{16,20},{20,24},{24,28},{1,5},{5,9},{9,... | collective-permute-start | bytes 1572872 | tf_op jit(solution)/shard_map/ppermute | solution.py:314
  66.6 36.1 %collective-permute-start.4 = (bf16[4,2,128,256]{3,2,1,0:T(8,128)(2,1)S(1)}, bf16[4,2,128,256]{3,2,1,0:T(8,128)(2,1)S(1)}, u32[]{:S(2)}, u32[]{:S(2)}) collective-permute-start(bf16[4,2,128,256]{3,2,1,0:T(8,128)(2,1)S(1)} %pad_maximum_fusion), channel_id=1, source_target_pairs={{4,0},{8,4},{12,8},{16,12},{20,16},{24,20},{28,24},{5,1},{9,5},{13... | collective-permute-start | bytes 1572872 | tf_op jit(solution)/shard_map/ppermute | solution.py:314
  73.4 29.4 %collective-permute-start.5 = (bf16[4,2,128,256]{3,2,1,0:T(8,128)(2,1)S(1)}, bf16[4,2,128,256]{3,2,1,0:T(8,128)(2,1)S(1)}, u32[]{:S(2)}, u32[]{:S(2)}) collective-permute-start(bf16[4,2,128,256]{3,2,1,0:T(8,128)(2,1)S(1)} %pad_maximum_fusion), channel_id=1, source_target_pairs={{8,0},{12,4},{16,8},{20,12},{24,16},{28,20},{9,1},{13,5},{17,9},{2... | collective-permute-start | bytes 1572872 | tf_op jit(solution)/shard_map/ppermute | solution.py:314
  90.7 28.8 %collective-permute-start.6 = (bf16[4,2,128,256]{3,2,1,0:T(8,128)(2,1)S(1)}, bf16[4,2,128,256]{3,2,1,0:T(8,128)(2,1)S(1)}, u32[]{:S(2)}, u32[]{:S(2)}) collective-permute-start(bf16[4,2,128,256]{3,2,1,0:T(8,128)(2,1)S(1)} %pad_maximum_fusion), channel_id=1, source_target_pairs={{12,0},{16,4},{20,8},{24,12},{28,16},{13,1},{17,5},{21,9},{25,13},... | collective-permute-start | bytes 1572872 | tf_op jit(solution)/shard_map/ppermute | solution.py:314
  101.2 45.1 %collective-permute-start.7 = (bf16[4,2,128,256]{3,2,1,0:T(8,128)(2,1)S(1)}, bf16[4,2,128,256]{3,2,1,0:T(8,128)(2,1)S(1)}, u32[]{:S(2)}, u32[]{:S(2)}) collective-permute-start(bf16[4,2,128,256]{3,2,1,0:T(8,128)(2,1)S(1)} %pad_maximum_fusion), channel_id=1, source_target_pairs={{16,0},{20,4},{24,8},{28,12},{17,1},{21,5},{25,9},{29,13},{18,2},{... | collective-permute-start | bytes 1572872 | tf_op jit(solution)/shard_map/ppermute | solution.py:314
  146.3 2.1 copy-start.1
Sparse Core Ops, SparseCore 0:
  8.9 37.1 all-gather.1
